TPU v7x, 32 devices: a whole 2x2x4 slice. The times are simulated.
32 devices in a mesh: fsdp: 8 (over z, x), island: 4 (over y, core).
Axes of the slice: x: 2, y: 2, z: 4, core: 2. Of those that a mesh axis runs over, the one named last changes fastest.
Arguments:
- acts: bfloat16 [4, 2048, 4096], P('island', 'fsdp'), may hold values from -6 to 6
- grad_out: bfloat16 [4, 2048, 128], P('island', 'fsdp'), may hold values from -0.52734375 to 0.52734375
- params: float32 [4, 4096, 128], P('island', 'fsdp'), may hold values from -3 to 3
- adam_m: float32 [4, 4096, 128], P('island', 'fsdp'), may hold values from -4 to 4
- adam_v: float32 [4, 4096, 128], P('island', 'fsdp'), may hold values from 0.01 to 16
- global_params: float32 [4096, 128], P('fsdp'), may hold values from -3 to 3
- outer_mom: float32 [4096, 128], P('fsdp'), may hold values from -2 to 2
Outputs:
- mixed: float32 [4, 4096, 128], P('island', 'fsdp')
- first_moment: float32 [4, 4096, 128], P('island', 'fsdp')
- second_moment: float32 [4, 4096, 128], P('island', 'fsdp')
- new_global: float32 [4096, 128], P('fsdp')
- new_mom: float32 [4096, 128], P('fsdp')
- forward_weight: bfloat16 [4, 4096, 128], P('island')
All inputs are finite; a program needn't handle non-finite values.
Results may differ from a plain program's by a relative error of at most 0.0004.
Values may be sent and summed in bfloat16 or wider, within the bound.
A program may use at most 64 MiB of HBM per device.

v0:
```python
import functools

import jax
import jax.numpy as jnp
from jax import lax
from jax.experimental import pallas as pl
from jax.experimental.pallas import tpu as pltpu
from jax.sharding import PartitionSpec as P

INNER_STEP = 100


beta_one = 0.9
beta_two = 0.95
epsilon = 1e-08
inner_rate = 0.001
decay_rate = 0.1
outer_rate = 0.7
momentum = 0.9
mixing = 0.5

CODE_SCALE = 4096.0
LAGS = (0, 0, 0, 0)
VMEM_LIMIT = 60 * 2**20


def encode(value):
    scaled = value * CODE_SCALE
    return (scaled * jnp.abs(scaled) * (scaled * scaled)).astype(jnp.bfloat16)


def decode(coded):
    wide = coded.astype(jnp.float32)
    size = jnp.maximum(jnp.abs(wide), 1e-37)
    root = lax.rsqrt(lax.rsqrt(size)) * (1.0 / CODE_SCALE)
    return jnp.where(wide < 0.0, -root, root)


def adam(params, adam_m, adam_v, gradient):
    first_moment = beta_one * adam_m + (1.0 - beta_one) * gradient
    second_moment = beta_two * adam_v + (1.0 - beta_two) * gradient * gradient
    first_hat = first_moment / (1.0 - beta_one**INNER_STEP)
    second_hat = second_moment / (1.0 - beta_two**INNER_STEP)
    inner = params - inner_rate * (
        first_hat / (jnp.sqrt(second_hat) + epsilon) + decay_rate * params
    )
    return first_moment, second_moment, inner


def kernel(
    ring, pairs, chunks, lags,
    acts_hbm, grad_hbm, params_hbm, m_hbm, v_hbm, global_hbm, mom_hbm,
    mixed_hbm, first_hbm, second_hbm, new_global_hbm, new_mom_hbm, forward_hbm,
    mixed, first_out, second_out, new_global, new_mom, forward,
    acts, grad_out, params, adam_m, adam_v, global_params, outer_mom,
    turned, part, r_out, r_in, inner, core_in, y_out, y_in,
    a_sem, i_sem, o_sem, w_sem, r_ss, r_rs, c_ss, c_rs, y_ss, y_rs, g_ss, g_rs,
):
    rows = params.shape[0]
    step = rows // chunks
    half = step // 2
    depth = ring // 2
    me = lax.axis_index("fsdp")
    isle = lax.axis_index("island")
    zi, xi = me // 2, lax.rem(me, 2)
    place = zi * (1 - xi) + (ring - 1 - zi) * xi
    pair, core = isle // 2, lax.rem(isle, 2)

    def index(k):
        spot = lax.rem(place + (k % ring), ring)
        side = spot // depth
        return (spot * (1 - side) + (ring - 1 - spot) * side) * 2 + side

    ahead = {"fsdp": index(1), "island": isle}
    behind = {"fsdp": index(-1), "island": isle}
    mate = {"fsdp": me, "island": pair * 2 + 1 - core}
    toward = (ahead, behind)

    def across(e, k):
        return {"fsdp": me, "island": lax.rem(pair + e, pairs) * 2 + k}

    barrier = pltpu.get_barrier_semaphore()
    peers = [ahead, behind, mate] + [across(e, k) for e in range(1, pairs) for k in range(2)]
    for peer in peers:
        pl.semaphore_signal(barrier, inc=1, device_id=peer, device_id_type=pl.DeviceIdType.MESH)

    def columns(k):
        return pl.ds(pl.multiple_of(index(k) * rows, rows), rows)

    def load(k):
        return pltpu.make_async_copy(
            acts_hbm.at[:, columns(k)], acts.at[k % ring], a_sem.at[k % ring]
        )

    singles = [
        (grad_hbm, grad_out), (params_hbm, params), (m_hbm, adam_m), (v_hbm, adam_v),
        (global_hbm, global_params), (mom_hbm, outer_mom),
    ]
    inputs = [pltpu.make_async_copy(s, d, i_sem.at[n]) for n, (s, d) in enumerate(singles)]
    needs = [depth]
    for k in range(depth - 1, 0, -1):
        needs += [k, ring - k]
    needs.append(0)
    inputs[0].start()
    for k in needs:
        load(k).start()
    for copy in inputs[1:]:
        copy.start()

    def product(k):
        load(k).wait()
        part[k] = jnp.dot(turned[...], acts[k], preferred_element_type=jnp.float32)

    def remote(src, dst, ss, rs, where):
        return pltpu.make_async_remote_copy(
            src_ref=src, dst_ref=dst, send_sem=ss, recv_sem=rs,
            device_id=where, device_id_type=pl.DeviceIdType.MESH,
        )

    def reach(c, q):
        return depth - (c + q) % 2

    def piece(c):
        return pl.ds(c * step, step)

    def r_copy(c, q, s):
        return remote(
            r_out.at[c, q, s], r_in.at[c, q, s], r_ss.at[c, q, s], r_rs.at[c, q, s], toward[q]
        )

    def c_copy(c):
        return remote(inner.at[piece(c)], core_in.at[c], c_ss.at[c], c_rs.at[c], mate)

    def y_copy(c, e, k):
        return remote(
            y_out.at[c, pl.ds(pl.multiple_of(core * half, half), half)],
            y_in.at[c, e, core], y_ss.at[c, e, k], y_rs.at[c, e, core], across(e, k),
        )

    def y_recv(c, e, k):
        return remote(
            y_out.at[c, pl.ds(0, half)], y_in.at[c, e, k],
            y_ss.at[c, e, k], y_rs.at[c, e, k], mate,
        )

    def g_copy(c, q, s, hop):
        k = hop if q else -hop
        first = pl.multiple_of(index(k) * rows + c * step, step)
        block = forward.at[pl.ds(first, step)]
        return remote(block, block, g_ss.at[c, q, s], g_rs.at[c, q, s], toward[q])

    landing = (
        (first_out, first_hbm), (second_out, second_hbm),
        (mixed, mixed_hbm), (new_global, new_global_hbm), (new_mom, new_mom_hbm),
    )

    def store(c, n):
        src, dst = landing[n]
        return pltpu.make_async_copy(src.at[piece(c)], dst.at[piece(c)], o_sem.at[c, n])

    def keep(c, q, hop):
        first = pl.multiple_of(index(hop if q else -hop) * rows + c * step, step)
        place_of = pl.ds(first, step)
        return pltpu.make_async_copy(
            forward.at[place_of], forward_hbm.at[place_of], w_sem.at[c, q, hop]
        )

    def sum_on(c, q, s):
        k = reach(c, q) - s
        value = part[(-k if q else k) % ring, :, piece(c)]
        if s > 0:
            r_copy(c, q, s - 1).wait_recv()
            value = value + decode(r_in[c, q, s - 1])
        r_out[c, q, s] = encode(value)
        r_copy(c, q, s).start()

    def reduce(c):
        total = part[0, :, piece(c)]
        for q in range(2):
            last = reach(c, q) - 1
            r_copy(c, q, last).wait_recv()
            total = total + decode(r_in[c, q, last])
        s = piece(c)
        first, second, own = adam(params[s], adam_m[s], adam_v[s], total.T)
        inner[s] = own
        c_copy(c).start()
        first_out[s] = first
        second_out[s] = second
        store(c, 0).start()
        store(c, 1).start()

    def join(c):
        c_copy(c).wait_recv()
        y_out[c] = inner[piece(c)] + core_in[c]
        for e in range(1, pairs):
            for k in range(2):
                y_copy(c, e, k).start()

    def outer(c):
        for e in range(1, pairs):
            for k in range(2):
                y_recv(c, e, k).wait_recv()
        for k in range(2):
            s = pl.ds(c * step + k * half, half)
            summed = y_out[c, pl.ds(k * half, half)]
            for e in range(1, pairs):
                summed = summed + y_in[c, e, k]
            delta = global_params[s] - summed / (2 * pairs)
            fresh = momentum * outer_mom[s] + delta
            moved = global_params[s] - outer_rate * (delta + momentum * fresh)
            merged = mixing * inner[s] + (1.0 - mixing) * moved
            first = pl.multiple_of(me * rows + c * step + k * half, half)
            forward[pl.ds(first, half)] = merged.astype(jnp.bfloat16)
            mixed[s] = merged
            new_mom[s] = fresh
            new_global[s] = moved
        for q in range(2):
            g_copy(c, q, 0, 0).start()
        keep(c, 0, 0).start()
        for n in range(2, 5):
            store(c, n).start()

    def pass_on(c, q, s):
        g_copy(c, q, s - 1, s).wait_recv()
        g_copy(c, q, s, s).start()
        keep(c, q, s).start()

    def tick(c, t):
        if t < depth:
            for q in range(2):
                if t < reach(c, q):
                    sum_on(c, q, t)
        elif t == depth:
            reduce(c)
        elif t == depth + 1:
            join(c)
        elif t == depth + 2:
            outer(c)
        else:
            for q in range(2):
                if t - depth - 2 < reach(c, q):
                    pass_on(c, q, t - depth - 2)

    inputs[0].wait()
    turned[...] = grad_out[...].T
    product(depth)
    pl.semaphore_wait(barrier, len(peers))
    for far in (depth, depth - 1):
        if far < depth:
            product(far)
            product(ring - far)
        for c in range(chunks):
            for q in range(2):
                if lags[c] == 0 and reach(c, q) == far:
                    sum_on(c, q, 0)
    for t in range(1, 2 * depth + 2 + max(lags)):
        if t < depth - 1:
            product(depth - 1 - t)
            product(depth + 1 + t)
        elif t == depth - 1:
            product(0)
            for copy in inputs[1:]:
                copy.wait()
        for c in range(chunks):
            if 0 <= t - lags[c] < 2 * depth + 2:
                tick(c, t - lags[c])

    for c in range(chunks):
        c_copy(c).wait_send()
        for e in range(1, pairs):
            for k in range(2):
                y_copy(c, e, k).wait_send()
        for q in range(2):
            for s in range(reach(c, q)):
                r_copy(c, q, s).wait_send()
                g_copy(c, q, s, s).wait_send()
            g_copy(c, q, reach(c, q) - 1, reach(c, q)).wait_recv()
            keep(c, q, reach(c, q)).start()
    for c in range(chunks):
        for n in range(5):
            store(c, n).wait()
        keep(c, 0, 0).wait()
        for q in range(2):
            for hop in range(1, reach(c, q) + 1):
                keep(c, q, hop).wait()


def write_out(parts, *refs):
    count = len(parts)
    sources, targets, held = refs[:count], refs[count : 2 * count], refs[2 * count : 3 * count]
    in_sem, out_sem = refs[3 * count :]
    loads, stores = [], []
    for n, cuts in enumerate(parts):
        extent = sources[n].shape[0] // cuts
        for cut in range(cuts):
            at = pl.ds(cut * extent, extent)
            spot = len(loads)
            loads.append(
                pltpu.make_async_copy(sources[n].at[at], held[n].at[at], in_sem.at[spot])
            )
            stores.append(
                pltpu.make_async_copy(held[n].at[at], targets[n].at[at], out_sem.at[spot])
            )
    for copy in loads:
        copy.start()
    for load, store in zip(loads, stores):
        load.wait()
        store.start()
    for copy in stores:
        copy.wait()


def fused(acts, grad_out, params, adam_m, adam_v, global_params, outer_mom):
    ring, islands = lax.axis_size("fsdp"), lax.axis_size("island")
    depth, pairs = ring // 2, islands // 2
    rows, width = params.shape[1:]
    tokens = acts.shape[1]
    chunks = len(LAGS)
    step = rows // chunks
    single = jax.ShapeDtypeStruct((rows, width), jnp.float32)
    whole = jax.ShapeDtypeStruct((ring * rows, width), jnp.bfloat16)
    dma = pltpu.SemaphoreType.DMA
    hbm = pl.BlockSpec(memory_space=pltpu.HBM)
    own = pltpu.VMEM((rows, width), jnp.float32)
    coded = pltpu.VMEM((chunks, 2, depth, width, step), jnp.bfloat16)
    results = pl.pallas_call(
        functools.partial(kernel, ring, pairs, chunks, LAGS),
        out_shape=[single] * 5 + [whole],
        in_specs=[hbm] * 7,
        out_specs=[hbm] * 6,
        scratch_shapes=[
            own, own, own, own, own,
            pltpu.VMEM((ring * rows, width), jnp.bfloat16),
            pltpu.VMEM((ring, tokens, rows), jnp.bfloat16),
            pltpu.VMEM((tokens, width), jnp.bfloat16),
            own, own, own, own, own,
            pltpu.VMEM((width, tokens), jnp.bfloat16),
            pltpu.VMEM((ring, width, rows), jnp.float32),
            coded, coded,
            own,
            pltpu.VMEM((chunks, step, width), jnp.float32),
            pltpu.VMEM((chunks, step, width), jnp.float32),
            pltpu.VMEM((chunks, pairs, 2, step // 2, width), jnp.float32),
            dma((ring,)), dma((6,)), dma((chunks, 5)), dma((chunks, 2, depth + 1)),
            dma((chunks, 2, depth)), dma((chunks, 2, depth)),
            dma((chunks,)), dma((chunks,)),
            dma((chunks, pairs, 2)), dma((chunks, pairs, 2)),
            dma((chunks, 2, depth)), dma((chunks, 2, depth)),
        ],
        compiler_params=pltpu.CompilerParams(
            collective_id=0, has_side_effects=True, vmem_limit_bytes=VMEM_LIMIT
        ),
    )(acts[0], grad_out[0], params[0], adam_m[0], adam_v[0], global_params, outer_mom)
    parts = (1,) * 5 + (4,)
    mixed, first, second, new_global, new_mom, forward = pl.pallas_call(
        functools.partial(write_out, parts),
        out_shape=[single] * 5 + [whole],
        in_specs=[hbm] * 6,
        out_specs=[hbm] * 6,
        scratch_shapes=[own] * 5 + [pltpu.VMEM(whole.shape, whole.dtype)] + [dma((sum(parts),))] * 2,
        compiler_params=pltpu.CompilerParams(vmem_limit_bytes=VMEM_LIMIT),
    )(*results)
    return mixed[None], first[None], second[None], new_global, new_mom, forward[None]


def general(acts, grad_out, params, adam_m, adam_v, global_params, outer_mom):
    shard_rows = params.shape[1]
    features = acts.shape[2]
    padded_rows = shard_rows * lax.axis_size("fsdp")
    islands = lax.axis_size("island")
    inputs = acts[0]
    cotangent = grad_out[0]
    whole = jnp.einsum("td,th->dh", inputs, cotangent, preferred_element_type=jnp.float32)
    whole = jnp.pad(whole, ((0, padded_rows - features), (0, 0)))
    gradient = lax.psum_scatter(whole, "fsdp", scatter_dimension=0, tiled=True)
    first_moment, second_moment, inner = adam(params, adam_m, adam_v, gradient[None])
    summed = lax.psum(inner, "island")
    delta = global_params - summed[0] / islands
    new_mom = momentum * outer_mom + delta
    new_global = global_params - outer_rate * (delta + momentum * new_mom)
    mixed = mixing * inner + (1.0 - mixing) * new_global[None]
    gathered = lax.all_gather(mixed.astype(jnp.bfloat16), "fsdp", axis=1, tiled=True)
    forward_weight = gathered[:, :features]
    return (mixed, first_moment, second_moment, new_global, new_mom, forward_weight)


def on_device(acts, *others):
    fsdp, islands = lax.axis_size("fsdp"), lax.axis_size("island")
    rows = others[1].shape[1]
    fits = (
        rows * fsdp == acts.shape[2]
        and rows % (len(LAGS) * 128) == 0
        and fsdp % 2 == 0
        and 2 <= fsdp // 2 <= 4
        and islands == 4
    )
    return (fused if fits else general)(acts, *others)


def solution(mesh):
    in_specs = (
        P("island", "fsdp", None),
        P("island", "fsdp", None),
        P("island", "fsdp", None),
        P("island", "fsdp", None),
        P("island", "fsdp", None),
        P("fsdp", None),
        P("fsdp", None),
    )
    out_specs = (
        P("island", "fsdp", None),
        P("island", "fsdp", None),
        P("island", "fsdp", None),
        P("fsdp", None),
        P("fsdp", None),
        P("island", None, None),
    )
    return jax.shard_map(
        on_device, mesh=mesh, in_specs=in_specs, out_specs=out_specs, check_vma=False
    )
```

profile of v0, /device:TPU:0, one launch (start us, length us, event | category | flops | bytes accessed | tf_op | source)
XLA Modules:
  0.0 45.4 jit_solution(2731195112296536264)
XLA Ops:
  0.6 42.3 %shard_map.118 = (f32[512,128]{1,0:T(8,128)}, f32[512,128]{1,0:T(8,128)}, f32[512,128]{1,0:T(8,128)}, f32[512,128]{1,0:T(8,128)}, f32[512,128]{1,0:T(8,128)}, /*index=5*/bf16[4096,128]{1,0:T(8,128)(2,1)}) custom-call(bf16[256,4096]{1,0:T(8,128)(2,1)} %bitcast.9, bf16[256,128]{1,0:T(8,128)(2,1)} %bitcast.13, f32[512,128]{1,0:T(8,128)} %bitcast.10, ...), custom_call_target="tpu_custom_call" | custom-call | tf_op jit(solution)/shard_map/pallas_call | solution.py:326
  42.9 2.5 %shard_map.119 = (f32[512,128]{1,0:T(8,128)}, f32[512,128]{1,0:T(8,128)}, f32[512,128]{1,0:T(8,128)}, f32[512,128]{1,0:T(8,128)}, f32[512,128]{1,0:T(8,128)}, /*index=5*/bf16[4096,128]{1,0:T(8,128)(2,1)}) custom-call(f32[512,128]{1,0:T(8,128)} %get-tuple-element.18.refs_0_, f32[512,128]{1,0:T(8,128)} %get-tuple-element.19.refs_1_, ...), custom_call_target="tpu_custom_call" | custom-call | tf_op jit(solution)/shard_map/pallas_call | solution.py:355
where the time goes:
time: 45.6 us; the launch traced here: 45.4 us
  Pallas kernels  44.8 us (98%)
  between operations  0.64 us (1%)
    pallas_call x1, Pallas kernels, fused(): pl.pallas_call(functools.partial(kernel, ring, pairs, chunks, LAGS), out_...  42.3 us
    pallas_call x1, Pallas kernels, fused(): pl.pallas_call(functools.partial(write_out, parts), out_shape=[single] *...  2.5 us

commit v1 on v0

--- a/solution.py
+++ b/solution.py
@@ -53,8 +53,8 @@
     mixed_hbm, first_hbm, second_hbm, new_global_hbm, new_mom_hbm, forward_hbm,
     mixed, first_out, second_out, new_global, new_mom, forward,
     acts, grad_out, params, adam_m, adam_v, global_params, outer_mom,
-    turned, part, r_out, r_in, inner, core_in, y_out, y_in,
-    a_sem, i_sem, o_sem, w_sem, r_ss, r_rs, c_ss, c_rs, y_ss, y_rs, g_ss, g_rs,
+    turned, part, r_out, r_in, inner, core_in, y_out, y_in, y_sum,
+    a_sem, i_sem, o_sem, w_sem, r_ss, r_rs, c_ss, c_rs, y_ss, y_rs, m_ss, m_rs, g_ss, g_rs,
 ):
     rows = params.shape[0]
     step = rows // chunks
@@ -76,11 +76,11 @@
     mate = {"fsdp": me, "island": pair * 2 + 1 - core}
     toward = (ahead, behind)
 
-    def across(e, k):
-        return {"fsdp": me, "island": lax.rem(pair + e, pairs) * 2 + k}
+    def across(e):
+        return {"fsdp": me, "island": lax.rem(pair + e, pairs) * 2 + core}
 
     barrier = pltpu.get_barrier_semaphore()
-    peers = [ahead, behind, mate] + [across(e, k) for e in range(1, pairs) for k in range(2)]
+    peers = [ahead, behind, mate] + [across(e) for e in range(1, pairs)]
     for peer in peers:
         pl.semaphore_signal(barrier, inc=1, device_id=peer, device_id_type=pl.DeviceIdType.MESH)
 
@@ -131,17 +131,17 @@
     def c_copy(c):
         return remote(inner.at[piece(c)], core_in.at[c], c_ss.at[c], c_rs.at[c], mate)
 
-    def y_copy(c, e, k):
+    def my_half():
+        return pl.ds(pl.multiple_of(core * half, half), half)
+
+    def y_copy(c, e):
         return remote(
-            y_out.at[c, pl.ds(pl.multiple_of(core * half, half), half)],
-            y_in.at[c, e, core], y_ss.at[c, e, k], y_rs.at[c, e, core], across(e, k),
+            y_out.at[c, my_half()], y_in.at[c, e], y_ss.at[c, e], y_rs.at[c, e], across(e)
         )
 
-    def y_recv(c, e, k):
-        return remote(
-            y_out.at[c, pl.ds(0, half)], y_in.at[c, e, k],
-            y_ss.at[c, e, k], y_rs.at[c, e, k], mate,
-        )
+    def m_copy(c):
+        block = y_sum.at[c, my_half()]
+        return remote(block, block, m_ss.at[c], m_rs.at[c], mate)
 
     def g_copy(c, q, s, hop):
         k = hop if q else -hop
@@ -193,18 +193,21 @@
         c_copy(c).wait_recv()
         y_out[c] = inner[piece(c)] + core_in[c]
         for e in range(1, pairs):
-            for k in range(2):
-                y_copy(c, e, k).start()
+            y_copy(c, e).start()
+
+    def swap(c):
+        total = y_out[c, my_half()]
+        for e in range(1, pairs):
+            y_copy(c, e).wait_recv()
+            total = total + y_in[c, e]
+        y_sum[c, my_half()] = total
+        m_copy(c).start()
 
     def outer(c):
-        for e in range(1, pairs):
-            for k in range(2):
-                y_recv(c, e, k).wait_recv()
+        m_copy(c).wait_recv()
         for k in range(2):
             s = pl.ds(c * step + k * half, half)
-            summed = y_out[c, pl.ds(k * half, half)]
-            for e in range(1, pairs):
-                summed = summed + y_in[c, e, k]
+            summed = y_sum[c, pl.ds(k * half, half)]
             delta = global_params[s] - summed / (2 * pairs)
             fresh = momentum * outer_mom[s] + delta
             moved = global_params[s] - outer_rate * (delta + momentum * fresh)
@@ -235,11 +238,13 @@
         elif t == depth + 1:
             join(c)
         elif t == depth + 2:
+            swap(c)
+        elif t == depth + 3:
             outer(c)
         else:
             for q in range(2):
-                if t - depth - 2 < reach(c, q):
-                    pass_on(c, q, t - depth - 2)
+                if t - depth - 3 < reach(c, q):
+                    pass_on(c, q, t - depth - 3)
 
     inputs[0].wait()
     turned[...] = grad_out[...].T
@@ -253,7 +258,7 @@
             for q in range(2):
                 if lags[c] == 0 and reach(c, q) == far:
                     sum_on(c, q, 0)
-    for t in range(1, 2 * depth + 2 + max(lags)):
+    for t in range(1, 2 * depth + 3 + max(lags)):
         if t < depth - 1:
             product(depth - 1 - t)
             product(depth + 1 + t)
@@ -262,27 +267,36 @@
             for copy in inputs[1:]:
                 copy.wait()
         for c in range(chunks):
-            if 0 <= t - lags[c] < 2 * depth + 2:
+            if 0 <= t - lags[c] < 2 * depth + 3:
                 tick(c, t - lags[c])
+        for c in range(chunks):
+            if t == depth + 4 + max(lags):
+                for q in range(2):
+                    for s in range(reach(c, q)):
+                        r_copy(c, q, s).wait_send()
+            if t == depth + 5 + max(lags):
+                c_copy(c).wait_send()
+                m_copy(c).wait_send()
+                for e in range(1, pairs):
+                    y_copy(c, e).wait_send()
+                for n in range(5):
+                    store(c, n).wait()
+                keep(c, 0, 0).wait()
+            if t == 2 * depth + 2 + max(lags):
+                for q in range(2):
+                    for s in range(reach(c, q) - 2):
+                        g_copy(c, q, s, s).wait_send()
+                        keep(c, q, s + 1).wait()
 
     for c in range(chunks):
-        c_copy(c).wait_send()
-        for e in range(1, pairs):
-            for k in range(2):
-                y_copy(c, e, k).wait_send()
         for q in range(2):
-            for s in range(reach(c, q)):
-                r_copy(c, q, s).wait_send()
-                g_copy(c, q, s, s).wait_send()
             g_copy(c, q, reach(c, q) - 1, reach(c, q)).wait_recv()
             keep(c, q, reach(c, q)).start()
     for c in range(chunks):
-        for n in range(5):
-            store(c, n).wait()
-        keep(c, 0, 0).wait()
         for q in range(2):
-            for hop in range(1, reach(c, q) + 1):
-                keep(c, q, hop).wait()
+            for s in range(reach(c, q) - 2, reach(c, q)):
+                g_copy(c, q, s, s).wait_send()
+                keep(c, q, s + 1).wait()
 
 
 def write_out(parts, *refs):
@@ -340,11 +354,13 @@
             own,
             pltpu.VMEM((chunks, step, width), jnp.float32),
             pltpu.VMEM((chunks, step, width), jnp.float32),
-            pltpu.VMEM((chunks, pairs, 2, step // 2, width), jnp.float32),
+            pltpu.VMEM((chunks, pairs, step // 2, width), jnp.float32),
+            pltpu.VMEM((chunks, step, width), jnp.float32),
             dma((ring,)), dma((6,)), dma((chunks, 5)), dma((chunks, 2, depth + 1)),
             dma((chunks, 2, depth)), dma((chunks, 2, depth)),
             dma((chunks,)), dma((chunks,)),
-            dma((chunks, pairs, 2)), dma((chunks, pairs, 2)),
+            dma((chunks, pairs)), dma((chunks, pairs)),
+            dma((chunks,)), dma((chunks,)),
             dma((chunks, 2, depth)), dma((chunks, 2, depth)),
         ],
         compiler_params=pltpu.CompilerParams(
@@ -391,7 +407,7 @@
         rows * fsdp == acts.shape[2]
         and rows % (len(LAGS) * 128) == 0
         and fsdp % 2 == 0
-        and 2 <= fsdp // 2 <= 4
+        and 3 <= fsdp // 2 <= 4
         and islands == 4
     )
     return (fused if fits else general)(acts, *others)

time: 45.6 us -> 45.7 us (level)
  no operation moved by 1% of the time
where the time goes in v1:
time: 45.7 us; the launch traced here: 45.5 us
  Pallas kernels  44.9 us (98%)
  between operations  0.64 us (1%)
    pallas_call x1, Pallas kernels, fused(): pl.pallas_call(functools.partial(kernel, ring, pairs, chunks, LAGS), out_...  42.4 us
    pallas_call x1, Pallas kernels, fused(): pl.pallas_call(functools.partial(write_out, parts), out_shape=[single] *...  2.5 us

profile of v1, /device:TPU:0, one launch (start us, length us, event | category | flops | bytes accessed | tf_op | source)
XLA Modules:
  0.0 45.5 jit_solution(140299321558894938)
XLA Ops:
  0.6 42.4 %shard_map.118 = (f32[512,128]{1,0:T(8,128)}, f32[512,128]{1,0:T(8,128)}, f32[512,128]{1,0:T(8,128)}, f32[512,128]{1,0:T(8,128)}, f32[512,128]{1,0:T(8,128)}, /*index=5*/bf16[4096,128]{1,0:T(8,128)(2,1)}) custom-call(bf16[256,4096]{1,0:T(8,128)(2,1)} %bitcast.9, bf16[256,128]{1,0:T(8,128)(2,1)} %bitcast.13, f32[512,128]{1,0:T(8,128)} %bitcast.10, ...), custom_call_target="tpu_custom_call" | custom-call | tf_op jit(solution)/shard_map/pallas_call | solution.py:340
  43.0 2.5 %shard_map.119 = (f32[512,128]{1,0:T(8,128)}, f32[512,128]{1,0:T(8,128)}, f32[512,128]{1,0:T(8,128)}, f32[512,128]{1,0:T(8,128)}, f32[512,128]{1,0:T(8,128)}, /*index=5*/bf16[4096,128]{1,0:T(8,128)(2,1)}) custom-call(f32[512,128]{1,0:T(8,128)} %get-tuple-element.18.refs_0_, f32[512,128]{1,0:T(8,128)} %get-tuple-element.19.refs_1_, ...), custom_call_target="tpu_custom_call" | custom-call | tf_op jit(solution)/shard_map/pallas_call | solution.py:371

commit v2 on v1

--- a/solution.py
+++ b/solution.py
@@ -20,7 +20,7 @@
 mixing = 0.5
 
 CODE_SCALE = 4096.0
-LAGS = (0, 0, 0, 0)
+LAGS = (0, 0)
 VMEM_LIMIT = 60 * 2**20
 
 

time: 45.7 us -> 47.2 us (1.033)
  Pallas kernels: 44.9 us -> 46.4 us
    pallas_call x1, Pallas kernels: 42.4 us -> 43.9 us  [fused(): pl.pallas_call(functools.partial(kernel, ring, pairs, chunks, LAGS), out_...]
where the time goes in v2:
time: 47.2 us; the launch traced here: 47 us
  Pallas kernels  46.4 us (98%)
  between operations  0.64 us (1%)
    pallas_call x1, Pallas kernels, fused(): pl.pallas_call(functools.partial(kernel, ring, pairs, chunks, LAGS), out_...  43.9 us
    pallas_call x1, Pallas kernels, fused(): pl.pallas_call(functools.partial(write_out, parts), out_shape=[single] *...  2.5 us

profile of v2, /device:TPU:0, one launch (start us, length us, event | category | flops | bytes accessed | tf_op | source)
XLA Modules:
  0.0 47.0 jit_solution(5291397048278917602)
XLA Ops:
  0.6 43.9 %shard_map.118 = (f32[512,128]{1,0:T(8,128)}, f32[512,128]{1,0:T(8,128)}, f32[512,128]{1,0:T(8,128)}, f32[512,128]{1,0:T(8,128)}, f32[512,128]{1,0:T(8,128)}, /*index=5*/bf16[4096,128]{1,0:T(8,128)(2,1)}) custom-call(bf16[256,4096]{1,0:T(8,128)(2,1)} %bitcast.9, bf16[256,128]{1,0:T(8,128)(2,1)} %bitcast.13, f32[512,128]{1,0:T(8,128)} %bitcast.10, ...), custom_call_target="tpu_custom_call" | custom-call | tf_op jit(solution)/shard_map/pallas_call | solution.py:340
  44.5 2.5 %shard_map.119 = (f32[512,128]{1,0:T(8,128)}, f32[512,128]{1,0:T(8,128)}, f32[512,128]{1,0:T(8,128)}, f32[512,128]{1,0:T(8,128)}, f32[512,128]{1,0:T(8,128)}, /*index=5*/bf16[4096,128]{1,0:T(8,128)(2,1)}) custom-call(f32[512,128]{1,0:T(8,128)} %get-tuple-element.18.refs_0_, f32[512,128]{1,0:T(8,128)} %get-tuple-element.19.refs_1_, ...), custom_call_target="tpu_custom_call" | custom-call | tf_op jit(solution)/shard_map/pallas_call | solution.py:371

commit v3 on v0

--- a/solution.py
+++ b/solution.py
@@ -20,7 +20,7 @@
 mixing = 0.5
 
 CODE_SCALE = 4096.0
-LAGS = (0, 0, 0, 0)
+LAGS = (0, 0, 1, 1)
 VMEM_LIMIT = 60 * 2**20
 
 

time: 45.6 us -> 46.6 us (1.022)
  Pallas kernels: 44.8 us -> 45.8 us
    pallas_call x1, Pallas kernels: 42.3 us -> 43.3 us  [fused(): pl.pallas_call(functools.partial(kernel, ring, pairs, chunks, LAGS), out_...]
where the time goes in v3:
time: 46.6 us; the launch traced here: 46.4 us
  Pallas kernels  45.8 us (98%)
  between operations  0.64 us (1%)
    pallas_call x1, Pallas kernels, fused(): pl.pallas_call(functools.partial(kernel, ring, pairs, chunks, LAGS), out_...  43.3 us
    pallas_call x1, Pallas kernels, fused(): pl.pallas_call(functools.partial(write_out, parts), out_shape=[single] *...  2.5 us

profile of v3, /device:TPU:0, one launch (start us, length us, event | category | flops | bytes accessed | tf_op | source)
XLA Modules:
  0.0 46.4 jit_solution(10569121449837728720)
XLA Ops:
  0.6 43.3 %shard_map.118 = (f32[512,128]{1,0:T(8,128)}, f32[512,128]{1,0:T(8,128)}, f32[512,128]{1,0:T(8,128)}, f32[512,128]{1,0:T(8,128)}, f32[512,128]{1,0:T(8,128)}, /*index=5*/bf16[4096,128]{1,0:T(8,128)(2,1)}) custom-call(bf16[256,4096]{1,0:T(8,128)(2,1)} %bitcast.9, bf16[256,128]{1,0:T(8,128)(2,1)} %bitcast.13, f32[512,128]{1,0:T(8,128)} %bitcast.10, ...), custom_call_target="tpu_custom_call" | custom-call | tf_op jit(solution)/shard_map/pallas_call | solution.py:326
  43.9 2.5 %shard_map.119 = (f32[512,128]{1,0:T(8,128)}, f32[512,128]{1,0:T(8,128)}, f32[512,128]{1,0:T(8,128)}, f32[512,128]{1,0:T(8,128)}, f32[512,128]{1,0:T(8,128)}, /*index=5*/bf16[4096,128]{1,0:T(8,128)(2,1)}) custom-call(f32[512,128]{1,0:T(8,128)} %get-tuple-element.18.refs_0_, f32[512,128]{1,0:T(8,128)} %get-tuple-element.19.refs_1_, ...), custom_call_target="tpu_custom_call" | custom-call | tf_op jit(solution)/shard_map/pallas_call | solution.py:355
